TPU v7x, 32 devices: a whole 2x2x4 slice. The times are simulated.
32 devices in a mesh: task: 4 (over y, x), width: 8 (over z, core).
Axes of the slice: x: 2, y: 2, z: 4, core: 2. Of those that a mesh axis runs over, the one named last changes fastest.
Arguments:
- task_ids: int32 [512], P('task'), may hold values from 0 to 1023
- embed_table: bfloat16 [1024, 1024], replicated, may hold values from -6 to 6
- trunk_weight: bfloat16 [1024, 2048], replicated, may hold values from -0.1875 to 0.1875
- trunk_bias: float32 [2048], replicated, may hold values from -6 to 6
- head_weight: bfloat16 [2048, 262144], P(None, ('task', 'width')), may hold values from -0.125 to 0.125
- head_bias: float32 [262144], P(('task', 'width')), may hold values from -4 to 4
- token_row: int32 [16384], P('task'), may hold values from 0 to 511, as said below
- inputs: bfloat16 [16384, 8192], P('task', 'width'), may hold values from -6 to 6
- frozen: bfloat16 [16384, 8192], P('task', 'width'), may hold values from -6 to 6
Outputs:
- adapted: bfloat16 [16384, 8192], P('task', 'width')
Inputs may be any that keep to these rules, and one draw needn't show every extreme that they name: `token_row`: each of the 512 rows is named by exactly 32 tokens, and tokens b * 4096 to (b + 1) * 4096 - 1 name only rows b * 128 to (b + 1) * 128 - 1.
All inputs are finite; a program needn't handle non-finite values.
Results may differ from a plain program's by a relative error of at most 0.0061.
Values may be sent and summed in bfloat16 or wider, within the bound.
A program may use at most 192 MiB of HBM per device.

v0:
```python
import math

import jax
import jax.numpy as jnp
from jax import lax
from jax.sharding import PartitionSpec as P

WIDTH = 8192
RANK = 16


def run_trunk(id_values, embed_table, trunk_weight, trunk_bias):
    one_hot = (
        id_values[:, None] == jnp.arange(embed_table.shape[0], dtype=jnp.int32)[None, :]
    ).astype(jnp.bfloat16)
    embedded = jnp.dot(one_hot, embed_table, preferred_element_type=jnp.float32).astype(
        jnp.bfloat16
    )
    preact = jnp.dot(embedded, trunk_weight, preferred_element_type=jnp.float32) + trunk_bias
    return jax.nn.silu(preact).astype(jnp.bfloat16)


def on_device(
    task_ids,
    embed_table,
    trunk_weight,
    trunk_bias,
    head_weight,
    head_bias,
    token_row,
    inputs,
    frozen,
):
    task_count = lax.axis_size("task")
    width_count = lax.axis_size("width")
    rows_dev = task_ids.shape[0]
    hidden = lax.all_gather(
        run_trunk(task_ids, embed_table, trunk_weight, trunk_bias), "task", axis=0, tiled=True
    )
    inner_cols = head_weight.shape[1] // width_count
    weight_cube = head_weight.reshape(head_weight.shape[0], inner_cols, width_count)
    hidden_rows = hidden.reshape(task_count, rows_dev, hidden.shape[1])
    head_out = jnp.einsum(
        "tqh,hks->qtsk", hidden_rows, weight_cube, preferred_element_type=jnp.float32
    )
    bias_grid = head_bias.reshape(inner_cols, width_count).T
    factors = (head_out + bias_grid[None, None, :, :]).astype(jnp.bfloat16)
    moved = lax.all_to_all(
        factors.reshape(rows_dev, task_count * width_count, inner_cols),
        ("task", "width"),
        split_axis=1,
        concat_axis=1,
        tiled=True,
    )
    slice_width = inputs.shape[1]
    grouped = moved.reshape(rows_dev, 2, RANK, slice_width)
    entry_flat = grouped[:, 0].reshape(rows_dev * RANK, slice_width)
    exit_flat = grouped[:, 1].reshape(rows_dev * RANK, slice_width)
    tok_count = inputs.shape[0]
    block_len = math.gcd(tok_count, 512)
    block_count = tok_count // block_len
    local_row = token_row - lax.axis_index("task") * rows_dev
    row_ids = jnp.arange(rows_dev, dtype=jnp.int32)
    input_blocks = inputs.reshape(block_count, block_len, slice_width)
    frozen_blocks = frozen.reshape(block_count, block_len, slice_width)
    row_blocks = local_row.reshape(block_count, block_len)

    def rank_block(block_data):
        tokens_in, rows_in = block_data
        selector = (rows_in[:, None] == row_ids[None, :]).astype(jnp.float32)
        scores = jnp.einsum("te,ke->tk", tokens_in, entry_flat, preferred_element_type=jnp.float32)
        return jnp.sum(scores.reshape(block_len, rows_dev, RANK) * selector[:, :, None], axis=1)

    rank_part = lax.map(rank_block, (input_blocks, row_blocks))
    rank_sum = lax.psum(rank_part, "width")
    rank_coef = (rank_sum * (1.0 / math.sqrt(WIDTH))).astype(jnp.bfloat16)

    def update_block(block_data):
        coef_in, frozen_in, rows_in = block_data
        selector = (rows_in[:, None] == row_ids[None, :]).astype(jnp.bfloat16)
        spread = (selector[:, :, None] * coef_in[:, None, :]).reshape(block_len, rows_dev * RANK)
        update = jnp.dot(spread, exit_flat, preferred_element_type=jnp.float32)
        return (frozen_in.astype(jnp.float32) + update * (1.0 / math.sqrt(RANK))).astype(
            jnp.bfloat16
        )

    result = lax.map(update_block, (rank_coef, frozen_blocks, row_blocks))
    return result.reshape(tok_count, slice_width)


def solution(mesh):
    return jax.shard_map(
        on_device,
        mesh=mesh,
        in_specs=(
            P("task"),
            P(),
            P(),
            P(),
            P(None, ("task", "width")),
            P(("task", "width")),
            P("task"),
            P("task", "width"),
            P("task", "width"),
        ),
        out_specs=P("task", "width"),
        check_vma=False,
    )
```

profile of v0, /device:TPU:0, one launch (start us, length us, event | category | flops | bytes accessed | tf_op | source)
XLA Modules:
  0.0 510.4 jit_solution(6610474896824235702)
XLA Ops:
  12.3 44.6 %copy.15 = bf16[2048,8192]{0,1:T(8,128)(2,1)} copy(bf16[2048,8192]{1,0:T(8,128)(2,1)} %param.17) | data formatting | bytes 67108864 | tf_op args[4]
  56.9 45.4 %copy.16 = bf16[2048,1024,8]{1,0,2:T(8,128)(2,1)} copy(bf16[2048,1024,8]{0,2,1:T(8,128)(2,1)} %bitcast.69) | data formatting | bytes 67108864 | tf_op jit(solution)/shard_map/reshape | solution.py:41
  102.7 26.0 %fusion.18 = bf16[128,4,8,1024]{3,0,2,1:T(8,128)(2,1)} fusion(bf16[4,128,2048,1]{2,1,3,0:T(8,128)(2,1)} %bitcast.80, bf16[2048,1024,8]{1,0,2:T(8,128)(2,1)} %copy.16, f32[8,1024]{1,0:T(8,128)S(1)} %copy.17), kind=kOutput, calls=%fused_computation.24 | convolution fusion | flops 17188257792 | bytes 44072960 | tf_op jit(solution)/shard_map/tqh,hks->qtsk/dot_general | solution.py:43
  128.8 6.8 %all-to-all-start = ((bf16[128,32,1024]{2,0,1:T(8,128)(2,1)}), bf16[128,32,1024]{2,0,1:T(8,128)(2,1)}, u32[]{:S(2)}, u32[]{:S(2)}) async-start(bf16[128,32,1024]{2,0,1:T(8,128)(2,1)} %bitcast.71), calls=%async_computation | async-start | bytes 16777216 | tf_op jit(solution)/shard_map/all_to_all | solution.py:48
  135.9 184.6 %all-to-all-done = bf16[128,32,1024]{2,0,1:T(8,128)(2,1)} async-done(((bf16[128,32,1024]{2,0,1:T(8,128)(2,1)}), bf16[128,32,1024]{2,0,1:T(8,128)(2,1)}, u32[]{:S(2)}, u32[]{:S(2)}) %all-to-all-start) | async-done | bytes 8388640 | tf_op jit(solution)/shard_map/all_to_all | solution.py:48
  330.1 69.8 %while.22 = (s32[]{:T(128)}, f32[8,512,16]{1,2,0:T(8,128)}, bf16[8,512,1024]{2,1,0:T(8,128)(2,1)}, bf16[2048,1024]{1,0:T(8,128)(2,1)}, s32[8,512]{1,0:T(8,128)S(1)}, /*index=5*/s32[]{:T(128)}) while((s32[]{:T(128)}, f32[8,512,16]{1,2,0:T(8,128)}, bf16[8,512,1024]{2,1,0:T(8,128)(2,1)}, bf16[2048,1024]{1,0:T(8,128)(2,1)}, ...), condition=%wide.region_2.3_spmd.clone, body=%wide.region_0.2_spmd.clone.sunk | while | flops 2149703680 | bytes 5872713 | solution.py:74
  330.2 8.1 %multiply_reduce_fusion.2 = f32[512,16]{0,1:T(8,128)S(1)} fusion(bf16[128,16,1024]{2,1,0:T(8,128)(2,1)} %bitcast.74, f32[512,128]{0,1:T(8,128)S(1)} %fusion.38, bf16[8,512,1024]{2,1,0:T(8,128)(2,1)} %get-tuple-element.208, s32[]{:T(128)} %get-tuple-element.200), kind=kOutput, calls=%fused_computation.4.clone.1 | convolution fusion | flops 2149572608 | bytes 5538304 | tf_op jit(solution)/shard_map/while/body/eval_jaxpr/te,ke->tk/dot_general | solution.py:71
  338.9 8.1 %multiply_reduce_fusion.2 = f32[512,16]{0,1:T(8,128)S(1)} fusion(bf16[128,16,1024]{2,1,0:T(8,128)(2,1)} %bitcast.74, f32[512,128]{0,1:T(8,128)S(1)} %fusion.38, bf16[8,512,1024]{2,1,0:T(8,128)(2,1)} %get-tuple-element.208, s32[]{:T(128)} %get-tuple-element.200), kind=kOutput, calls=%fused_computation.4.clone.1 | convolution fusion | flops 2149572608 | bytes 5538304 | tf_op jit(solution)/shard_map/while/body/eval_jaxpr/te,ke->tk/dot_general | solution.py:71
  347.6 8.1 %multiply_reduce_fusion.2 = f32[512,16]{0,1:T(8,128)S(1)} fusion(bf16[128,16,1024]{2,1,0:T(8,128)(2,1)} %bitcast.74, f32[512,128]{0,1:T(8,128)S(1)} %fusion.38, bf16[8,512,1024]{2,1,0:T(8,128)(2,1)} %get-tuple-element.208, s32[]{:T(128)} %get-tuple-element.200), kind=kOutput, calls=%fused_computation.4.clone.1 | convolution fusion | flops 2149572608 | bytes 5538304 | tf_op jit(solution)/shard_map/while/body/eval_jaxpr/te,ke->tk/dot_general | solution.py:71
  356.3 8.1 %multiply_reduce_fusion.2 = f32[512,16]{0,1:T(8,128)S(1)} fusion(bf16[128,16,1024]{2,1,0:T(8,128)(2,1)} %bitcast.74, f32[512,128]{0,1:T(8,128)S(1)} %fusion.38, bf16[8,512,1024]{2,1,0:T(8,128)(2,1)} %get-tuple-element.208, s32[]{:T(128)} %get-tuple-element.200), kind=kOutput, calls=%fused_computation.4.clone.1 | convolution fusion | flops 2149572608 | bytes 5538304 | tf_op jit(solution)/shard_map/while/body/eval_jaxpr/te,ke->tk/dot_general | solution.py:71
  365.1 8.1 %multiply_reduce_fusion.2 = f32[512,16]{0,1:T(8,128)S(1)} fusion(bf16[128,16,1024]{2,1,0:T(8,128)(2,1)} %bitcast.74, f32[512,128]{0,1:T(8,128)S(1)} %fusion.38, bf16[8,512,1024]{2,1,0:T(8,128)(2,1)} %get-tuple-element.208, s32[]{:T(128)} %get-tuple-element.200), kind=kOutput, calls=%fused_computation.4.clone.1 | convolution fusion | flops 2149572608 | bytes 5538304 | tf_op jit(solution)/shard_map/while/body/eval_jaxpr/te,ke->tk/dot_general | solution.py:71
  373.8 8.1 %multiply_reduce_fusion.2 = f32[512,16]{0,1:T(8,128)S(1)} fusion(bf16[128,16,1024]{2,1,0:T(8,128)(2,1)} %bitcast.74, f32[512,128]{0,1:T(8,128)S(1)} %fusion.38, bf16[8,512,1024]{2,1,0:T(8,128)(2,1)} %get-tuple-element.208, s32[]{:T(128)} %get-tuple-element.200), kind=kOutput, calls=%fused_computation.4.clone.1 | convolution fusion | flops 2149572608 | bytes 5538304 | tf_op jit(solution)/shard_map/while/body/eval_jaxpr/te,ke->tk/dot_general | solution.py:71
  382.5 8.1 %multiply_reduce_fusion.2 = f32[512,16]{0,1:T(8,128)S(1)} fusion(bf16[128,16,1024]{2,1,0:T(8,128)(2,1)} %bitcast.74, f32[512,128]{0,1:T(8,128)S(1)} %fusion.38, bf16[8,512,1024]{2,1,0:T(8,128)(2,1)} %get-tuple-element.208, s32[]{:T(128)} %get-tuple-element.200), kind=kOutput, calls=%fused_computation.4.clone.1 | convolution fusion | flops 2149572608 | bytes 5538304 | tf_op jit(solution)/shard_map/while/body/eval_jaxpr/te,ke->tk/dot_general | solution.py:71
  391.2 8.1 %multiply_reduce_fusion.2 = f32[512,16]{0,1:T(8,128)S(1)} fusion(bf16[128,16,1024]{2,1,0:T(8,128)(2,1)} %bitcast.74, f32[512,128]{0,1:T(8,128)S(1)} %fusion.38, bf16[8,512,1024]{2,1,0:T(8,128)(2,1)} %get-tuple-element.208, s32[]{:T(128)} %get-tuple-element.200), kind=kOutput, calls=%fused_computation.4.clone.1 | convolution fusion | flops 2149572608 | bytes 5538304 | tf_op jit(solution)/shard_map/while/body/eval_jaxpr/te,ke->tk/dot_general | solution.py:71
  399.9 6.5 %copy.22 = bf16[128,1,16,1024]{3,2,0,1:T(8,128)(2,1)} copy(bf16[128,1,16,1024]{3,0,2,1:T(8,128)(2,1)} %get-tuple-element.124) | data formatting | bytes 8388608
  406.4 46.2 %all-reduce.2.cloned.1.call-done = f32[8,512,16]{1,2,0:T(8,128)} async-done(((f32[8,512,16]{1,2,0:T(8,128)}), f32[8,512,16]{1,2,0:T(8,128)}) %all-reduce.2.cloned.1.call-update) | async-done | bytes 262160 | tf_op jit(solution)/shard_map/psum | solution.py:75
  453.6 48.5 %while.23 = (s32[]{:T(128)}, bf16[8,512,1024]{2,1,0:T(8,128)(2,1)}, bf16[8,512,1024]{2,1,0:T(8,128)(2,1)}, s32[8,512]{1,0:T(8,128)S(1)}, bf16[8,512,16]{1,2,0:T(...) while((s32[]{:T(128)}, bf16[8,512,1024]{2,1,0:T(8,128)(2,1)}, ...), condition=%wide.region_5.6_spmd.clone, body=%wide.region_4.5_spmd.clone.sunk | while | flops 2150760448 | bytes 10803797 | solution.py:87
  453.8 5.8 %fusion.42 = bf16[8,512,1024]{2,1,0:T(8,128)(2,1)} fusion(bf16[8,512,1024]{2,1,0:T(8,128)(2,1)} %get-tuple-element.220, s32[]{:T(128)} %get-tuple-element.219, bf16[512,2048]{0,1:T(8,128)(2,1)S(1)} %bitcast.70, bf16[2048,1024]{1,0:T(8,128)(2,1)} %get-tuple-element.231, bf16[8,512,1024]{2,1,0:T(8,128)(2,1)} %get-tuple-element.228), kind=kOutput, calls=%fused_computation.15.clone.1 | convolution fusion | flops 2149580800 | bytes 8389120 | tf_op jit(solution)/shard_map/while/body/eval_jaxpr/dot_general | solution.py:82
  459.9 5.8 %fusion.42 = bf16[8,512,1024]{2,1,0:T(8,128)(2,1)} fusion(bf16[8,512,1024]{2,1,0:T(8,128)(2,1)} %get-tuple-element.220, s32[]{:T(128)} %get-tuple-element.219, bf16[512,2048]{0,1:T(8,128)(2,1)S(1)} %bitcast.70, bf16[2048,1024]{1,0:T(8,128)(2,1)} %get-tuple-element.231, bf16[8,512,1024]{2,1,0:T(8,128)(2,1)} %get-tuple-element.228), kind=kOutput, calls=%fused_computation.15.clone.1 | convolution fusion | flops 2149580800 | bytes 8389120 | tf_op jit(solution)/shard_map/while/body/eval_jaxpr/dot_general | solution.py:82
  465.9 5.8 %fusion.42 = bf16[8,512,1024]{2,1,0:T(8,128)(2,1)} fusion(bf16[8,512,1024]{2,1,0:T(8,128)(2,1)} %get-tuple-element.220, s32[]{:T(128)} %get-tuple-element.219, bf16[512,2048]{0,1:T(8,128)(2,1)S(1)} %bitcast.70, bf16[2048,1024]{1,0:T(8,128)(2,1)} %get-tuple-element.231, bf16[8,512,1024]{2,1,0:T(8,128)(2,1)} %get-tuple-element.228), kind=kOutput, calls=%fused_computation.15.clone.1 | convolution fusion | flops 2149580800 | bytes 8389120 | tf_op jit(solution)/shard_map/while/body/eval_jaxpr/dot_general | solution.py:82
  472.0 5.8 %fusion.42 = bf16[8,512,1024]{2,1,0:T(8,128)(2,1)} fusion(bf16[8,512,1024]{2,1,0:T(8,128)(2,1)} %get-tuple-element.220, s32[]{:T(128)} %get-tuple-element.219, bf16[512,2048]{0,1:T(8,128)(2,1)S(1)} %bitcast.70, bf16[2048,1024]{1,0:T(8,128)(2,1)} %get-tuple-element.231, bf16[8,512,1024]{2,1,0:T(8,128)(2,1)} %get-tuple-element.228), kind=kOutput, calls=%fused_computation.15.clone.1 | convolution fusion | flops 2149580800 | bytes 8389120 | tf_op jit(solution)/shard_map/while/body/eval_jaxpr/dot_general | solution.py:82
  478.0 5.8 %fusion.42 = bf16[8,512,1024]{2,1,0:T(8,128)(2,1)} fusion(bf16[8,512,1024]{2,1,0:T(8,128)(2,1)} %get-tuple-element.220, s32[]{:T(128)} %get-tuple-element.219, bf16[512,2048]{0,1:T(8,128)(2,1)S(1)} %bitcast.70, bf16[2048,1024]{1,0:T(8,128)(2,1)} %get-tuple-element.231, bf16[8,512,1024]{2,1,0:T(8,128)(2,1)} %get-tuple-element.228), kind=kOutput, calls=%fused_computation.15.clone.1 | convolution fusion | flops 2149580800 | bytes 8389120 | tf_op jit(solution)/shard_map/while/body/eval_jaxpr/dot_general | solution.py:82
  484.1 5.8 %fusion.42 = bf16[8,512,1024]{2,1,0:T(8,128)(2,1)} fusion(bf16[8,512,1024]{2,1,0:T(8,128)(2,1)} %get-tuple-element.220, s32[]{:T(128)} %get-tuple-element.219, bf16[512,2048]{0,1:T(8,128)(2,1)S(1)} %bitcast.70, bf16[2048,1024]{1,0:T(8,128)(2,1)} %get-tuple-element.231, bf16[8,512,1024]{2,1,0:T(8,128)(2,1)} %get-tuple-element.228), kind=kOutput, calls=%fused_computation.15.clone.1 | convolution fusion | flops 2149580800 | bytes 8389120 | tf_op jit(solution)/shard_map/while/body/eval_jaxpr/dot_general | solution.py:82
  490.1 5.8 %fusion.42 = bf16[8,512,1024]{2,1,0:T(8,128)(2,1)} fusion(bf16[8,512,1024]{2,1,0:T(8,128)(2,1)} %get-tuple-element.220, s32[]{:T(128)} %get-tuple-element.219, bf16[512,2048]{0,1:T(8,128)(2,1)S(1)} %bitcast.70, bf16[2048,1024]{1,0:T(8,128)(2,1)} %get-tuple-element.231, bf16[8,512,1024]{2,1,0:T(8,128)(2,1)} %get-tuple-element.228), kind=kOutput, calls=%fused_computation.15.clone.1 | convolution fusion | flops 2149580800 | bytes 8389120 | tf_op jit(solution)/shard_map/while/body/eval_jaxpr/dot_general | solution.py:82
  (80 shorter events, 31.4 us)
Async XLA Ops:
  6.5 1.6 copy-start
  6.5 96.2 %all-gather.2.cloned.1.call-start = ((), (), s32[]{:S(2)}) async-start(), calls=%async_computation.1 | async-start | bytes 2621440 | tf_op jit(solution)/shard_map/all_gather | solution.py:37
  56.9 45.4 %copy-start.2 = (f32[8192]{0:T(1024)S(1)}, f32[8192]{0:T(1024)}, u32[]{:S(2)}) copy-start(f32[8192]{0:T(1024)} %param.18) | copy-start | bytes 98308
  128.8 7.1 %copy-start.3 = (s32[4096]{0:T(1024)S(1)}, s32[4096]{0:T(1024)}, u32[]{:S(2)}) copy-start(s32[4096]{0:T(1024)} %param.19) | copy-start | bytes 49156
  128.8 191.8 %all-to-all-start = ((bf16[128,32,1024]{2,0,1:T(8,128)(2,1)}), bf16[128,32,1024]{2,0,1:T(8,128)(2,1)}, u32[]{:S(2)}, u32[]{:S(2)}) async-start(bf16[128,32,1024]{2,0,1:T(8,128)(2,1)} %bitcast.71), calls=%async_computation | async-start | bytes 16777216 | tf_op jit(solution)/shard_map/all_to_all | solution.py:48
  135.6 316.9 %all-reduce.2.cloned.1.call-start = ((), (), s32[]{:S(2)}) async-start(), calls=%async_computation.2 | async-start | bytes 524288 | tf_op jit(solution)/shard_map/psum | solution.py:75
  502.0 1.6 copy-start.1
Sparse Core Ops, SparseCore 0:
  12.4 38.0 all-gather.1
  400.1 52.4 all-reduce.1
where the time goes:
time: 513 us; the launch traced here: 510 us
  waiting for transfers between devices  231 us (45%)
  matrix products  141 us (27%)
  local copies, waits for them, and re-layouts  115 us (22%)
  between operations  13.5 us (3%)
  starting transfers between devices  7.07 us (1%)
    all_to_all x1, waiting for transfers between devices, on_device(): lax.all_to_all(factors.reshape(rows_dev, task_count * width_count, inner_...  185 us
    dot_general x8, matrix products, rank_block(): jnp.einsum('te,ke->tk', tokens_in, entry_flat, preferred_element_type=jnp...  64.5 us
    unnamed x11, local copies, waits for them, and re-layouts  58.6 us
    dot_general x8, matrix products, update_block(): update = jnp.dot(spread, exit_flat, preferred_element_type=jnp.float32)  46.5 us
    psum x1, waiting for transfers between devices, on_device(): rank_sum = lax.psum(rank_part, 'width')  46.2 us
    reshape x1, local copies, waits for them, and re-layouts, on_device(): head_weight.reshape(head_weight.shape[0], inner_cols, width_count)  45.4 us
    dot_general x1, matrix products, on_device(): jnp.einsum('tqh,hks->qtsk', hidden_rows, weight_cube, preferred_element_t...  26 us
  transfers between devices with their start and end apart: 3, of which 2 were waited for; matrix products, arithmetic and copies ran while one was open for 19% of the time, Pallas kernels for 0%

commit v1 on v0

v1 whole, which is shorter than its diff:
```python
import functools
import math

import jax
import jax.numpy as jnp
from jax import lax
from jax.experimental import pallas as pl
from jax.experimental.pallas import tpu as pltpu
from jax.sharding import PartitionSpec as P

WIDTH = 8192
RANK = 16
MESH = pl.DeviceIdType.MESH
F32 = jnp.float32
BF16 = jnp.bfloat16


def exchange_kernel(
    dims,
    ids_ref,
    table_hbm,
    trunk_hbm,
    trunk_bias_ref,
    head_hbm,
    head_bias_ref,
    token_ref,
    inputs_hbm,
    factors,
    coef_out,
    ids_all,
    table,
    trunk,
    one_hot,
    hidden,
    weight,
    perm,
    flat,
    outgoing,
    stage,
    entry,
    tokens,
    part,
    gathered,
    coef_all,
    ids_send,
    ids_recv,
    hop_send,
    hop_recv,
    wide_send,
    wide_recv,
    part_send,
    part_recv,
    coef_send,
    coef_recv,
    load_sem,
    weight_sem,
    token_sem,
):
    task_count, width_count, rows, inner, slice_width, step_cols, steps, block = dims
    cols = step_cols * width_count
    task = lax.axis_index("task")
    wide = lax.axis_index("width")
    entry_tasks = [t for t in range(task_count) if t * width_count * inner < RANK * slice_width]
    exit_tasks = [t for t in range(task_count) if t not in entry_tasks]

    def weight_copy(step):
        return pltpu.make_async_copy(
            head_hbm.at[:, pl.ds(pl.multiple_of(step * cols, cols), cols)],
            weight.at[lax.rem(step, weight.shape[0])],
            weight_sem.at[lax.rem(step, weight.shape[0])],
        )

    def token_copy(index):
        return pltpu.make_async_copy(
            inputs_hbm.at[pl.ds(pl.multiple_of(index * block, block), block)],
            tokens.at[lax.rem(index, 2)],
            token_sem.at[lax.rem(index, 2)],
        )

    table_copy = pltpu.make_async_copy(table_hbm, table, load_sem.at[0])
    trunk_copy = pltpu.make_async_copy(trunk_hbm, trunk, load_sem.at[1])
    table_copy.start()
    trunk_copy.start()
    weight_copy(0).start()

    barrier = pltpu.get_barrier_semaphore()
    for d in range(1, task_count):
        pl.semaphore_signal(
            barrier,
            inc=1,
            device_id=(lax.rem(task + d, task_count), wide),
            device_id_type=MESH,
        )
    for d in range(1, width_count):
        pl.semaphore_signal(
            barrier,
            inc=1,
            device_id=(task, lax.rem(wide + d, width_count)),
            device_id_type=MESH,
        )

    ids_all[task] = jnp.broadcast_to(ids_ref[...], (8, rows))
    place = lax.broadcasted_iota(jnp.int32, (1, cols), 1)
    source = (place % step_cols) * width_count + place // step_cols
    for top in range(0, cols, 256):
        down = lax.broadcasted_iota(jnp.int32, (256, cols), 0) + top
        perm[top : top + 256, :] = jnp.where(down == source, 1.0, 0.0).astype(BF16)

    pl.semaphore_wait(barrier, task_count + width_count - 2)

    def ids_copy(peer, slot):
        return pltpu.make_async_remote_copy(
            src_ref=ids_all.at[slot],
            dst_ref=ids_all.at[slot],
            send_sem=ids_send.at[peer],
            recv_sem=ids_recv.at[slot],
            device_id=(peer, wide),
            device_id_type=MESH,
        )

    for d in range(1, task_count):
        ids_copy(lax.rem(task + d, task_count), task).start()
    for d in range(1, task_count):
        ids_copy(lax.rem(task + d, task_count), lax.rem(task + d, task_count)).wait_recv()
    for d in range(1, task_count):
        ids_copy(lax.rem(task + d, task_count), task).wait_send()

    table_len = table.shape[0]
    for t in range(task_count):
        spread_ids = jnp.transpose(jnp.broadcast_to(ids_all[t, 0:1, :], (128, rows)))
        lane = lax.broadcasted_iota(jnp.int32, (rows, 128), 1)
        for k in range(0, table_len, 128):
            one_hot[t * rows : (t + 1) * rows, k : k + 128] = jnp.where(
                spread_ids == lane + k, 1.0, 0.0
            ).astype(BF16)
    table_copy.wait()
    embedded = jnp.dot(one_hot[...], table[...], preferred_element_type=F32).astype(BF16)
    trunk_copy.wait()
    tile = 512
    for k in range(0, trunk.shape[1], tile):
        pre = (
            jnp.dot(embedded, trunk[:, k : k + tile], preferred_element_type=F32)
            + trunk_bias_ref[:, k : k + tile]
        )
        hidden[:, k : k + tile] = (pre / (1.0 + jnp.exp(-pre))).astype(BF16)

    def target(source_task, source_wide, step):
        place = (source_task * width_count + source_wide) * inner + step * step_cols
        return factors.at[
            place // slice_width,
            :,
            pl.ds(pl.multiple_of(lax.rem(place, slice_width), step_cols), step_cols),
        ]

    def hop_copy(peer, source_task, step):
        return pltpu.make_async_remote_copy(
            src_ref=outgoing.at[step, peer],
            dst_ref=stage.at[source_task, step],
            send_sem=hop_send.at[peer, step],
            recv_sem=hop_recv.at[source_task, step],
            device_id=(peer, wide),
            device_id_type=MESH,
        )

    def send_wide(blocks, source_task, step):
        for d in range(1, width_count):
            peer = lax.rem(wide + d, width_count)
            pltpu.make_async_remote_copy(
                src_ref=blocks.at[peer],
                dst_ref=target(source_task, wide, step),
                send_sem=wide_send.at[source_task, step],
                recv_sem=wide_recv.at[source_task, step],
                device_id=(task, peer),
                device_id_type=MESH,
            ).start()
        pltpu.make_async_copy(
            blocks.at[wide], target(source_task, wide, step), wide_recv.at[source_task, step]
        ).start()

    def head_step(step, carry):
        weight_copy(step).wait()

        @pl.when(step + 1 < steps)
        def _():
            weight_copy(step + 1).start()

        slot = lax.rem(step, weight.shape[0])
        for k in range(0, cols, 256):
            total = jnp.dot(
                hidden[...], weight[slot, :, k : k + 256], preferred_element_type=F32
            )
            flat[:, k : k + 256] = (total + head_bias_ref[step, :, k : k + 256]).astype(BF16)
        for k in range(0, cols, 256):
            sorted_cols = jnp.dot(
                flat[...], perm[:, k : k + 256], preferred_element_type=F32
            ).astype(BF16)
            for s in range(0, 256, step_cols):
                for t in range(task_count):
                    outgoing[step, t, (k + s) // step_cols] = sorted_cols[
                        t * rows : (t + 1) * rows, s : s + step_cols
                    ]
        for d in range(1, task_count):
            hop_copy(lax.rem(task + d, task_count), task, step).start()
        send_wide(outgoing.at[step, task], task, step)
        return carry

    lax.fori_loop(0, steps, head_step, 0)
    token_copy(0).start()

    def forward(sources):
        def body(step, carry):
            for t in sources:

                @pl.when(task != t)
                def _():
                    hop_copy(t, t, step).wait_recv()
                    send_wide(stage.at[t, step], t, step)

            return carry

        lax.fori_loop(0, steps, body, 0)

    forward(entry_tasks)
    forward(exit_tasks)

    def wait_wide(sources):
        def body(step, carry):
            for t in sources:
                whole = stage.at[t, step]
                pltpu.make_async_copy(whole, whole, wide_recv.at[t, step]).wait()
            return carry

        lax.fori_loop(0, steps, body, 0)

    wait_wide(entry_tasks)
    entry_copy = pltpu.make_async_copy(factors.at[pl.ds(0, RANK)], entry, load_sem.at[0])
    entry_copy.start()
    entry_copy.wait()

    def part_copy(peer, slot):
        return pltpu.make_async_remote_copy(
            src_ref=part.at[peer],
            dst_ref=gathered.at[slot],
            send_sem=part_send.at[peer],
            recv_sem=part_recv.at[slot],
            device_id=(task, peer),
            device_id_type=MESH,
        )

    def score_block(index, carry):
        token_copy(index).wait()

        @pl.when(index + 1 < width_count)
        def _():
            token_copy(index + 1).start()

        local = token_ref[index] - task * rows
        chosen = lax.broadcasted_iota(jnp.int32, (rows, block), 0) == local
        block_in = tokens[lax.rem(index, 2)]
        half = RANK // 2
        for top in range(0, RANK, half):
            scores = lax.dot_general(
                entry[top : top + half].reshape(half * rows, slice_width),
                block_in,
                (((1,), (1,)), ((), ())),
                preferred_element_type=F32,
            ).reshape(half, rows, block)
            part[index, top : top + half] = jnp.sum(
                jnp.where(chosen[None], scores, 0.0), axis=1
            )

        @pl.when(index != wide)
        def _():
            part_copy(index, wide).start()

        return carry

    lax.fori_loop(0, width_count, score_block, 0)
    total = part[wide]
    for d in range(1, width_count):
        peer = lax.rem(wide + d, width_count)
        part_copy(peer, peer).wait_recv()
        total = total + gathered[peer]
    coef_all[wide] = (total * (1.0 / math.sqrt(WIDTH))).astype(BF16)

    def coef_copy(peer, slot):
        return pltpu.make_async_remote_copy(
            src_ref=coef_all.at[slot],
            dst_ref=coef_all.at[slot],
            send_sem=coef_send.at[peer],
            recv_sem=coef_recv.at[slot],
            device_id=(task, peer),
            device_id_type=MESH,
        )

    for d in range(1, width_count):
        coef_copy(lax.rem(wide + d, width_count), wide).start()
    for d in range(1, width_count):
        peer = lax.rem(wide + d, width_count)
        coef_copy(peer, peer).wait_recv()
    coef_out[...] = coef_all[...]

    for d in range(1, width_count):
        peer = lax.rem(wide + d, width_count)
        part_copy(peer, peer).wait_send()
        coef_copy(peer, wide).wait_send()

    def drain(step, carry):
        for d in range(1, task_count):
            hop_copy(lax.rem(task + d, task_count), task, step).wait_send()
        for t in range(task_count):
            sent = stage.at[t, step, pl.ds(0, width_count - 1)]
            pltpu.make_async_copy(sent, sent, wide_send.at[t, step]).wait()
        return carry

    lax.fori_loop(0, steps, drain, 0)
    wait_wide(exit_tasks)


def update_kernel(rows, token_ref, coef_ref, exit_ref, frozen_ref, out_ref):
    local = token_ref[0] - lax.axis_index("task") * rows
    block = local.shape[1]
    spread_ids = jnp.transpose(jnp.broadcast_to(local, (128, block)))
    chosen = spread_ids == lax.broadcasted_iota(jnp.int32, (block, 128), 1)
    coef = jnp.transpose(coef_ref[0].astype(F32))
    spread = jnp.concatenate(
        [jnp.where(chosen, coef[:, r : r + 1], 0.0).astype(BF16)[:, :rows] for r in range(RANK)],
        axis=1,
    )
    exit_flat = exit_ref[...].reshape(RANK * rows, exit_ref.shape[2])
    tile = min(512, exit_ref.shape[2])
    for k in range(0, exit_ref.shape[2], tile):
        update = jnp.dot(spread, exit_flat[:, k : k + tile], preferred_element_type=F32)
        out_ref[:, k : k + tile] = (
            frozen_ref[:, k : k + tile].astype(F32) + update * (1.0 / math.sqrt(RANK))
        ).astype(BF16)


def on_device(
    task_ids,
    embed_table,
    trunk_weight,
    trunk_bias,
    head_weight,
    head_bias,
    token_row,
    inputs,
    frozen,
):
    task_count = lax.axis_size("task")
    width_count = lax.axis_size("width")
    rows = task_ids.shape[0]
    hid = trunk_weight.shape[1]
    inner = head_weight.shape[1] // width_count
    tok_count, slice_width = inputs.shape
    step_cols = 128
    steps = inner // step_cols
    cols = step_cols * width_count
    block = tok_count // width_count
    dims = (task_count, width_count, rows, inner, slice_width, step_cols, steps, block)
    all_rows = task_count * rows
    token_blocks = token_row.reshape(width_count, 1, block)
    vmem = pl.BlockSpec(memory_space=pltpu.VMEM)
    hbm = pl.BlockSpec(memory_space=pl.ANY)
    dma = pltpu.SemaphoreType.DMA
    factors, coef = pl.pallas_call(
        functools.partial(exchange_kernel, dims),
        out_shape=(
            jax.ShapeDtypeStruct((2 * RANK, rows, slice_width), BF16),
            jax.ShapeDtypeStruct((width_count, RANK, block), BF16),
        ),
        in_specs=[vmem, hbm, hbm, vmem, hbm, vmem, vmem, hbm],
        out_specs=(hbm, vmem),
        scratch_shapes=[
            pltpu.VMEM((task_count, 8, rows), jnp.int32),
            pltpu.VMEM(embed_table.shape, BF16),
            pltpu.VMEM(trunk_weight.shape, BF16),
            pltpu.VMEM((all_rows, embed_table.shape[0]), BF16),
            pltpu.VMEM((all_rows, hid), BF16),
            pltpu.VMEM((min(2, steps), hid, cols), BF16),
            pltpu.VMEM((cols, cols), BF16),
            pltpu.VMEM((all_rows, cols), BF16),
            pltpu.VMEM((steps, task_count, width_count, rows, step_cols), BF16),
            pltpu.VMEM((task_count, steps, width_count, rows, step_cols), BF16),
            pltpu.VMEM((RANK, rows, slice_width), BF16),
            pltpu.VMEM((2, block, slice_width), BF16),
            pltpu.VMEM((width_count, RANK, block), F32),
            pltpu.VMEM((width_count, RANK, block), F32),
            pltpu.VMEM((width_count, RANK, block), BF16),
            dma((task_count,)),
            dma((task_count,)),
            dma((task_count, steps)),
            dma((task_count, steps)),
            dma((task_count, steps)),
            dma((task_count, steps)),
            dma((width_count,)),
            dma((width_count,)),
            dma((width_count,)),
            dma((width_count,)),
            dma((2,)),
            dma((2,)),
            dma((2,)),
        ],
        compiler_params=pltpu.CompilerParams(
            collective_id=0, has_side_effects=True, vmem_limit_bytes=58 * 1024 * 1024
        ),
        name="factor_exchange",
    )(
        task_ids.reshape(1, rows),
        embed_table,
        trunk_weight,
        trunk_bias.reshape(1, hid),
        head_weight,
        head_bias.reshape(steps, 1, cols),
        token_blocks,
        inputs,
    )
    return pl.pallas_call(
        functools.partial(update_kernel, rows),
        grid=(width_count,),
        out_shape=jax.ShapeDtypeStruct((tok_count, slice_width), BF16),
        in_specs=[
            pl.BlockSpec((1, 1, block), lambda i: (i, 0, 0)),
            pl.BlockSpec((1, RANK, block), lambda i: (i, 0, 0)),
            pl.BlockSpec((RANK, rows, slice_width), lambda i: (1, 0, 0)),
            pl.BlockSpec((block, slice_width), lambda i: (i, 0)),
        ],
        out_specs=pl.BlockSpec((block, slice_width), lambda i: (i, 0)),
        compiler_params=pltpu.CompilerParams(vmem_limit_bytes=48 * 1024 * 1024),
        name="apply_update",
    )(token_blocks, coef, factors, frozen)


def solution(mesh):
    return jax.shard_map(
        on_device,
        mesh=mesh,
        in_specs=(
            P("task"),
            P(),
            P(),
            P(),
            P(None, ("task", "width")),
            P(("task", "width")),
            P("task"),
            P("task", "width"),
            P("task", "width"),
        ),
        out_specs=P("task", "width"),
        check_vma=False,
    )
```

time: 513 us -> 242 us (0.47)
  Pallas kernels: 0 us -> 240 us
  waiting for transfers between devices: 231 us -> 0 us
  matrix products: 141 us -> 0 us
  local copies, waits for them, and re-layouts: 115 us -> 0.9 us
  between operations: 13.5 us -> 0.03 us
  starting transfers between devices: 7.07 us -> 0 us
    pallas_call x0 -> x2, Pallas kernels: none -> 240 us  [the longest x1 216 us: on_device(): pl.pallas_call(functools.partial(exchange_kernel, dims), out_shape=(jax.S...]
    all_to_all x1 -> x0, waiting for transfers between devices: 185 us -> none  [on_device(): lax.all_to_all(factors.reshape(rows_dev, task_count * width_count, inner_...]
    dot_general x18 -> x0, matrix products: 141 us -> none  [the longest x8 64.5 us: rank_block(): jnp.einsum('te,ke->tk', tokens_in, entry_flat, preferred_element_type=jnp...]
    unnamed x11 -> x4, local copies, waits for them, and re-layouts: 58.6 us -> 0.9 us
    psum x1 -> x0, waiting for transfers between devices: 46.2 us -> none  [on_device(): rank_sum = lax.psum(rank_part, 'width')]
    reshape x3 -> x0, local copies, waits for them, and re-layouts: 45.7 us -> none  [the longest x1 45.4 us: on_device(): head_weight.reshape(head_weight.shape[0], inner_cols, width_count)]
    all_to_all x1 -> x0, starting transfers between devices: 6.85 us -> none  [on_device(): lax.all_to_all(factors.reshape(rows_dev, task_count * width_count, inner_...]
    slice x1 -> x0, local copies, waits for them, and re-layouts: 5.25 us -> none  [on_device(): exit_flat = grouped[:, 1].reshape(rows_dev * RANK, slice_width)]
  transfers between devices with their start and end apart: 3 -> 0, of which waited for: 2 -> 0; matrix products, arithmetic and copies ran while one was open for 19% -> 0% of each run, Pallas kernels for 0% -> 0%
where the time goes in v1:
time: 242 us; the launch traced here: 241 us
  Pallas kernels  240 us (99%)
    pallas_call x1, Pallas kernels, on_device(): pl.pallas_call(functools.partial(exchange_kernel, dims), out_shape=(jax.S...  216 us
    pallas_call x1, Pallas kernels, on_device(): pl.pallas_call(functools.partial(update_kernel, rows), grid=(width_count,...  24 us

profile of v1, /device:TPU:0, one launch (start us, length us, event | category | flops | bytes accessed | tf_op | source)
XLA Modules:
  0.0 241.4 jit_solution(7609878161171053893)
XLA Ops:
  0.0 0.0 copy-start.1
  0.0 216.5 %factor_exchange.1 = (bf16[32,128,1024]{2,1,0:T(8,128)(2,1)}, bf16[8,16,512]{2,1,0:T(8,128)(2,1)}) custom-call(s32[1,128]{1,0:T(1,128)} %bitcast.8, bf16[1024,1024]{1,0:T(8,128)(2,1)} %table_hbm.1, bf16[1024,2048]{1,0:T(8,128)(2,1)} %trunk_hbm.1, f32[1,2048]{1,0:T(1,128)} %bitcast.7, bf16[2048,8192]{1,0:T(8,128)(2,1)} %head_hbm.1, f32[8,1,1024]{2,1,0:T(1,128)} %bitcast.6, ...), custom_call_target="tpu_custom_call" | custom-call | tf_op jit(solution)/shard_map/factor_exchange/pallas_call | solution.py:366
  216.5 0.0 copy-done.1
  216.5 0.0 copy-start
  216.5 0.9 copy-done
  217.4 24.0 %apply_update.1 = bf16[4096,1024]{1,0:T(8,128)(2,1)} custom-call(s32[8,1,512]{2,1,0:T(1,128)S(1)} %bitcast.5, bf16[8,16,512]{2,1,0:T(8,128)(2,1)S(1)} %copy-done, bf16[32,128,1024]{2,1,0:T(8,128)(2,1)} %get-tuple-element.8.exit_ref, bf16[4096,1024]{1,0:T(8,128)(2,1)} %frozen_ref.1), custom_call_target="tpu_custom_call" | custom-call | tf_op jit(solution)/shard_map/apply_update/pallas_call | solution.py:418
Async XLA Ops:
  0.0 216.5 %copy-start.1 = (s32[4096]{0:T(1024)S(1)}, s32[4096]{0:T(1024)}, u32[]{:S(2)}) copy-start(s32[4096]{0:T(1024)} %param.15) | copy-start | bytes 49156
  216.5 0.9 copy-start

commit v2 on v1

v2 whole, which is shorter than its diff:
```python
import functools
import math

import jax
import jax.numpy as jnp
from jax import lax
from jax.experimental import pallas as pl
from jax.experimental.pallas import tpu as pltpu
from jax.sharding import PartitionSpec as P

WIDTH = 8192
RANK = 16
MESH = pl.DeviceIdType.MESH
F32 = jnp.float32
BF16 = jnp.bfloat16


def exchange_kernel(
    dims,
    ids_ref,
    table_hbm,
    trunk_hbm,
    trunk_bias_ref,
    head_hbm,
    head_bias_ref,
    token_ref,
    inputs_hbm,
    frozen_hbm,
    out_hbm,
    factors,
    ids_all,
    outgoing,
    stage,
    part,
    gathered,
    coef_all,
    ids_send,
    ids_recv,
    hop_send,
    hop_recv,
    wide_send,
    wide_recv,
    part_send,
    part_recv,
    coef_send,
    coef_recv,
    load_sem,
    weight_sem,
    token_sem,
    frozen_sem,
    out_sem,
):
    task_count, width_count, rows, inner, slice_width, step_cols, steps, block = dims
    cols = step_cols * width_count
    task = lax.axis_index("task")
    wide = lax.axis_index("width")
    entry_tasks = [t for t in range(task_count) if t * width_count * inner < RANK * slice_width]
    exit_tasks = [t for t in range(task_count) if t not in entry_tasks]

    hid = trunk_hbm.shape[1]
    all_rows = task_count * rows

    def partner(distance):
        if width_count & (width_count - 1):
            return lax.rem(wide + distance, width_count)
        peer = wide
        for bit in range(width_count.bit_length() - 1):
            if (distance >> bit) & 1:
                peer = peer + (1 << bit) * (1 - 2 * lax.rem(wide // (1 << bit), 2))
        return peer

    def target(source_task, source_wide, step):
        place = (source_task * width_count + source_wide) * inner + step * step_cols
        return factors.at[
            place // slice_width,
            :,
            pl.ds(pl.multiple_of(lax.rem(place, slice_width), step_cols), step_cols),
        ]

    def hop_copy(peer, source_task, step):
        return pltpu.make_async_remote_copy(
            src_ref=outgoing.at[step, peer],
            dst_ref=stage.at[source_task, step],
            send_sem=hop_send.at[peer, step],
            recv_sem=hop_recv.at[source_task, step],
            device_id=(peer, wide),
            device_id_type=MESH,
        )

    def send_wide(blocks, source_task, step):
        for d in reversed(range(1, width_count)):
            peer = partner(d)
            pltpu.make_async_remote_copy(
                src_ref=blocks.at[peer],
                dst_ref=target(source_task, wide, step),
                send_sem=wide_send.at[source_task, step],
                recv_sem=wide_recv.at[source_task, step],
                device_id=(task, peer),
                device_id_type=MESH,
            ).start()
        pltpu.make_async_copy(
            blocks.at[wide], target(source_task, wide, step), wide_recv.at[source_task, step]
        ).start()

    def forward(sources, step):
        for t in sources:

            @pl.when(task != t)
            def _():
                hop_copy(t, t, step).wait_recv()
                send_wide(stage.at[t, step], t, step)

    def forward_all(sources, first):
        def body(step, carry):
            forward(sources, step)
            return carry

        lax.fori_loop(first, steps, body, 0)

    def wait_wide(sources, step):
        for t in sources:
            whole = stage.at[t, step]
            pltpu.make_async_copy(whole, whole, wide_recv.at[t, step]).wait()

    def wait_wide_all(sources):
        def body(step, carry):
            wait_wide(sources, step)
            return carry

        lax.fori_loop(0, steps, body, 0)

    lag = 5
    early = max(0, steps - lag)

    def generate(table, trunk, one_hot, hidden, weight, perm, flat):
        def weight_copy(step):
            return pltpu.make_async_copy(
                head_hbm.at[:, pl.ds(pl.multiple_of(step * cols, cols), cols)],
                weight.at[lax.rem(step, weight.shape[0])],
                weight_sem.at[lax.rem(step, weight.shape[0])],
            )

        table_copy = pltpu.make_async_copy(table_hbm, table, load_sem.at[0])
        trunk_copy = pltpu.make_async_copy(trunk_hbm, trunk, load_sem.at[1])
        table_copy.start()
        trunk_copy.start()
        weight_copy(0).start()

        barrier = pltpu.get_barrier_semaphore()
        for d in range(1, task_count):
            pl.semaphore_signal(
                barrier,
                inc=1,
                device_id=(lax.rem(task + d, task_count), wide),
                device_id_type=MESH,
            )
        for d in range(1, width_count):
            pl.semaphore_signal(
                barrier,
                inc=1,
                device_id=(task, lax.rem(wide + d, width_count)),
                device_id_type=MESH,
            )

        ids_all[task] = jnp.broadcast_to(ids_ref[...], (8, rows))
        place = lax.broadcasted_iota(jnp.int32, (1, cols), 1)
        source = (place % step_cols) * width_count + place // step_cols
        for top in range(0, cols, 256):
            down = lax.broadcasted_iota(jnp.int32, (256, cols), 0) + top
            perm[top : top + 256, :] = jnp.where(down == source, 1.0, 0.0).astype(BF16)

        pl.semaphore_wait(barrier, task_count + width_count - 2)

        def ids_copy(peer, slot):
            return pltpu.make_async_remote_copy(
                src_ref=ids_all.at[slot],
                dst_ref=ids_all.at[slot],
                send_sem=ids_send.at[peer],
                recv_sem=ids_recv.at[slot],
                device_id=(peer, wide),
                device_id_type=MESH,
            )

        for d in range(1, task_count):
            ids_copy(lax.rem(task + d, task_count), task).start()
        for d in range(1, task_count):
            ids_copy(lax.rem(task + d, task_count), lax.rem(task + d, task_count)).wait_recv()
        for d in range(1, task_count):
            ids_copy(lax.rem(task + d, task_count), task).wait_send()

        table_len = table.shape[0]
        for t in range(task_count):
            spread_ids = jnp.transpose(jnp.broadcast_to(ids_all[t, 0:1, :], (128, rows)))
            lane = lax.broadcasted_iota(jnp.int32, (rows, 128), 1)
            for k in range(0, table_len, 128):
                one_hot[t * rows : (t + 1) * rows, k : k + 128] = jnp.where(
                    spread_ids == lane + k, 1.0, 0.0
                ).astype(BF16)
        table_copy.wait()
        embedded = jnp.dot(one_hot[...], table[...], preferred_element_type=F32).astype(BF16)
        trunk_copy.wait()
        tile = 512
        for k in range(0, trunk.shape[1], tile):
            pre = (
                jnp.dot(embedded, trunk[:, k : k + tile], preferred_element_type=F32)
                + trunk_bias_ref[:, k : k + tile]
            )
            hidden[:, k : k + tile] = (pre / (1.0 + jnp.exp(-pre))).astype(BF16)

        def head_step(step, carry):
            weight_copy(step).wait()

            @pl.when(step + 1 < steps)
            def _():
                weight_copy(step + 1).start()

            slot = lax.rem(step, weight.shape[0])
            for k in range(0, cols, 256):
                total = jnp.dot(
                    hidden[...], weight[slot, :, k : k + 256], preferred_element_type=F32
                )
                flat[:, k : k + 256] = (total + head_bias_ref[step, :, k : k + 256]).astype(BF16)
            for k in range(0, cols, 256):
                sorted_cols = jnp.dot(
                    flat[...], perm[:, k : k + 256], preferred_element_type=F32
                ).astype(BF16)
                for s in range(0, 256, step_cols):
                    for t in range(task_count):
                        outgoing[step, t, (k + s) // step_cols] = sorted_cols[
                            t * rows : (t + 1) * rows, s : s + step_cols
                        ]
            for d in range(1, task_count):
                hop_copy(lax.rem(task + d, task_count), task, step).start()
            send_wide(outgoing.at[step, task], task, step)
            if early:

                @pl.when(step >= lag)
                def _():
                    forward(entry_tasks, step - lag)

            return carry

        lax.fori_loop(0, steps, head_step, 0)

    pl.run_scoped(
        generate,
        pltpu.VMEM(table_hbm.shape, BF16),
        pltpu.VMEM(trunk_hbm.shape, BF16),
        pltpu.VMEM((all_rows, table_hbm.shape[0]), BF16),
        pltpu.VMEM((all_rows, hid), BF16),
        pltpu.VMEM((min(2, steps), hid, cols), BF16),
        pltpu.VMEM((cols, cols), BF16),
        pltpu.VMEM((all_rows, cols), BF16),
    )
    forward_all(entry_tasks, early)
    forward_all(exit_tasks, 0)
    wait_wide_all(entry_tasks)

    def part_copy(peer, slot):
        return pltpu.make_async_remote_copy(
            src_ref=part.at[peer],
            dst_ref=gathered.at[slot],
            send_sem=part_send.at[peer],
            recv_sem=part_recv.at[slot],
            device_id=(task, peer),
            device_id_type=MESH,
        )

    def rank(entry, tokens):
        def token_copy(index):
            return pltpu.make_async_copy(
                inputs_hbm.at[pl.ds(pl.multiple_of(index * block, block), block)],
                tokens.at[lax.rem(index, 2)],
                token_sem.at[lax.rem(index, 2)],
            )

        token_copy(0).start()
        entry_copy = pltpu.make_async_copy(factors.at[pl.ds(0, RANK)], entry, load_sem.at[0])
        entry_copy.start()
        entry_copy.wait()

        def score_block(index, carry):
            token_copy(index).wait()

            @pl.when(index + 1 < width_count)
            def _():
                token_copy(index + 1).start()

            local = token_ref[index] - task * rows
            chosen = lax.broadcasted_iota(jnp.int32, (rows, block), 0) == local
            block_in = tokens[lax.rem(index, 2)]
            half = RANK // 2
            for top in range(0, RANK, half):
                scores = lax.dot_general(
                    entry[top : top + half].reshape(half * rows, slice_width),
                    block_in,
                    (((1,), (1,)), ((), ())),
                    preferred_element_type=F32,
                ).reshape(half, rows, block)
                part[index, top : top + half] = jnp.sum(
                    jnp.where(chosen[None], scores, 0.0), axis=1
                )

            @pl.when(index != wide)
            def _():
                part_copy(index, wide).start()

            return carry

        lax.fori_loop(0, width_count, score_block, 0)

    pl.run_scoped(
        rank,
        pltpu.VMEM((RANK, rows, slice_width), BF16),
        pltpu.VMEM((2, block, slice_width), BF16),
    )
    total = part[wide]
    for d in range(1, width_count):
        peer = lax.rem(wide + d, width_count)
        part_copy(peer, peer).wait_recv()
        total = total + gathered[peer]
    coef_all[wide] = (total * (1.0 / math.sqrt(WIDTH))).astype(BF16)

    def coef_copy(peer, slot):
        return pltpu.make_async_remote_copy(
            src_ref=coef_all.at[slot],
            dst_ref=coef_all.at[slot],
            send_sem=coef_send.at[peer],
            recv_sem=coef_recv.at[slot],
            device_id=(task, peer),
            device_id_type=MESH,
        )

    for d in range(1, width_count):
        coef_copy(lax.rem(wide + d, width_count), wide).start()
    for d in range(1, width_count):
        peer = lax.rem(wide + d, width_count)
        coef_copy(peer, peer).wait_recv()
    chunk = min(256, slice_width)
    aligned = inner % slice_width == 0 and chunk % step_cols == 0

    def update(spread, exit_buf, frozen_buf, out_buf):
        def columns(array, index):
            return array.at[:, pl.ds(pl.multiple_of(index * chunk, chunk), chunk)]

        def frozen_copy(index):
            slot = lax.rem(index, 2)
            return pltpu.make_async_copy(
                columns(frozen_hbm, index), frozen_buf.at[slot], frozen_sem.at[slot]
            )

        def out_copy(index):
            slot = lax.rem(index, 2)
            return pltpu.make_async_copy(
                out_buf.at[slot], columns(out_hbm, index), out_sem.at[slot]
            )

        frozen_copy(0).start()

        def spread_block(index, carry):
            local = token_ref[index] - task * rows
            spread_ids = jnp.transpose(jnp.broadcast_to(local, (128, block)))
            chosen = spread_ids == lax.broadcasted_iota(jnp.int32, (block, 128), 1)
            coef = jnp.transpose(coef_all[index].astype(F32))
            place = pl.ds(pl.multiple_of(index * block, block), block)
            for r in range(RANK):
                piece = jnp.where(chosen, coef[:, r : r + 1], 0.0).astype(BF16)
                spread[place, r * rows : (r + 1) * rows] = piece[:, :rows]
            return carry

        lax.fori_loop(0, width_count, spread_block, 0)
        count = slice_width // chunk
        if not aligned:
            wait_wide_all(exit_tasks)

        def update_chunk(index, carry):
            slot = lax.rem(index, 2)

            @pl.when(index + 1 < count)
            def _():
                frozen_copy(index + 1).start()

            if aligned:
                per = chunk // step_cols
                for turn in range(inner // slice_width):
                    for q in range(per):
                        wait_wide(
                            exit_tasks, turn * (slice_width // step_cols) + index * per + q
                        )
            exit_copy = pltpu.make_async_copy(
                factors.at[
                    pl.ds(RANK, RANK), :, pl.ds(pl.multiple_of(index * chunk, chunk), chunk)
                ],
                exit_buf,
                load_sem.at[1],
            )
            exit_copy.start()
            frozen_copy(index).wait()

            @pl.when(index >= 2)
            def _():
                out_copy(index - 2).wait()

            exit_copy.wait()

            def token_block(row_block, inner_carry):
                place = pl.ds(pl.multiple_of(row_block * block, block), block)
                change = jnp.dot(
                    spread[place, :],
                    exit_buf[...].reshape(RANK * rows, chunk),
                    preferred_element_type=F32,
                )
                out_buf[slot, place, :] = (
                    frozen_buf[slot, place, :].astype(F32) + change * (1.0 / math.sqrt(RANK))
                ).astype(BF16)
                return inner_carry

            lax.fori_loop(0, width_count, token_block, 0)
            out_copy(index).start()
            return carry

        lax.fori_loop(0, count, update_chunk, 0)
        for index in range(max(0, count - 2), count):
            out_copy(index).wait()

    tok_count = width_count * block
    pl.run_scoped(
        update,
        pltpu.VMEM((tok_count, RANK * rows), BF16),
        pltpu.VMEM((RANK, rows, chunk), BF16),
        pltpu.VMEM((2, tok_count, chunk), BF16),
        pltpu.VMEM((2, tok_count, chunk), BF16),
    )

    for d in range(1, width_count):
        peer = lax.rem(wide + d, width_count)
        part_copy(peer, peer).wait_send()
        coef_copy(peer, wide).wait_send()

    def drain(step, carry):
        for d in range(1, task_count):
            hop_copy(lax.rem(task + d, task_count), task, step).wait_send()
        for t in range(task_count):
            sent = stage.at[t, step, pl.ds(0, width_count - 1)]
            pltpu.make_async_copy(sent, sent, wide_send.at[t, step]).wait()
        return carry

    lax.fori_loop(0, steps, drain, 0)


def on_device(
    task_ids,
    embed_table,
    trunk_weight,
    trunk_bias,
    head_weight,
    head_bias,
    token_row,
    inputs,
    frozen,
):
    task_count = lax.axis_size("task")
    width_count = lax.axis_size("width")
    rows = task_ids.shape[0]
    hid = trunk_weight.shape[1]
    inner = head_weight.shape[1] // width_count
    tok_count, slice_width = inputs.shape
    step_cols = 128
    steps = inner // step_cols
    cols = step_cols * width_count
    block = tok_count // width_count
    dims = (task_count, width_count, rows, inner, slice_width, step_cols, steps, block)
    token_blocks = token_row.reshape(width_count, 1, block)
    vmem = pl.BlockSpec(memory_space=pltpu.VMEM)
    hbm = pl.BlockSpec(memory_space=pl.ANY)
    dma = pltpu.SemaphoreType.DMA
    out, _ = pl.pallas_call(
        functools.partial(exchange_kernel, dims),
        out_shape=(
            jax.ShapeDtypeStruct((tok_count, slice_width), BF16),
            jax.ShapeDtypeStruct((2 * RANK, rows, slice_width), BF16),
        ),
        in_specs=[vmem, hbm, hbm, vmem, hbm, vmem, vmem, hbm, hbm],
        out_specs=(hbm, hbm),
        scratch_shapes=[
            pltpu.VMEM((task_count, 8, rows), jnp.int32),
            pltpu.VMEM((steps, task_count, width_count, rows, step_cols), BF16),
            pltpu.VMEM((task_count, steps, width_count, rows, step_cols), BF16),
            pltpu.VMEM((width_count, RANK, block), F32),
            pltpu.VMEM((width_count, RANK, block), F32),
            pltpu.VMEM((width_count, RANK, block), BF16),
            dma((task_count,)),
            dma((task_count,)),
            dma((task_count, steps)),
            dma((task_count, steps)),
            dma((task_count, steps)),
            dma((task_count, steps)),
            dma((width_count,)),
            dma((width_count,)),
            dma((width_count,)),
            dma((width_count,)),
            dma((2,)),
            dma((2,)),
            dma((2,)),
            dma((2,)),
            dma((2,)),
        ],
        compiler_params=pltpu.CompilerParams(
            collective_id=0, has_side_effects=True, vmem_limit_bytes=58 * 1024 * 1024
        ),
        name="adapt_rows",
    )(
        task_ids.reshape(1, rows),
        embed_table,
        trunk_weight,
        trunk_bias.reshape(1, hid),
        head_weight,
        head_bias.reshape(steps, 1, cols),
        token_blocks,
        inputs,
        frozen,
    )
    return out


def solution(mesh):
    return jax.shard_map(
        on_device,
        mesh=mesh,
        in_specs=(
            P("task"),
            P(),
            P(),
            P(),
            P(None, ("task", "width")),
            P(("task", "width")),
            P("task"),
            P("task", "width"),
            P("task", "width"),
        ),
        out_specs=P("task", "width"),
        check_vma=False,
    )
```

time: 242 us -> 264 us (1.091)
  Pallas kernels: 240 us -> 256 us
  local copies, waits for them, and re-layouts: 0.9 us -> 7.76 us
    pallas_call x1, Pallas kernels: 216 us -> 256 us  [on_device(): pl.pallas_call(functools.partial(exchange_kernel, dims), out_shape=(jax.S...]
    pallas_call x1 -> x0, Pallas kernels: 24 us -> none  [on_device(): pl.pallas_call(functools.partial(update_kernel, rows), grid=(width_count,...]
    unnamed x4 -> x1, local copies, waits for them, and re-layouts: 0.9 us -> 7.76 us
where the time goes in v2:
time: 264 us
  Pallas kernels  256 us (97%)
  local copies, waits for them, and re-layouts  7.76 us (3%)
    pallas_call x1, Pallas kernels, on_device(): pl.pallas_call(functools.partial(exchange_kernel, dims), out_shape=(jax.S...  256 us
    unnamed x1, local copies, waits for them, and re-layouts  7.76 us

profile of v2, /device:TPU:0, one launch (start us, length us, event | category | flops | bytes accessed | tf_op | source)
XLA Modules:
  0.0 263.9 jit_solution(8776675648796641633)
XLA Ops:
  0.0 256.1 %adapt_rows.1 = (bf16[4096,1024]{1,0:T(8,128)(2,1)}, bf16[32,128,1024]{2,1,0:T(8,128)(2,1)}) custom-call(s32[1,128]{1,0:T(1,128)} %bitcast.7, bf16[1024,1024]{1,0:T(8,128)(2,1)} %table_hbm.1, bf16[1024,2048]{1,0:T(8,128)(2,1)} %trunk_hbm.1, f32[1,2048]{1,0:T(1,128)} %bitcast.6, bf16[2048,8192]{1,0:T(8,128)(2,1)} %head_hbm.1, f32[8,1,1024]{2,1,0:T(1,128)} %bitcast.4, ...), custom_call_target="tpu_custom_call" | custom-call | tf_op jit(solution)/shard_map/adapt_rows/pallas_call | solution.py:477
  256.2 7.8 %copy.11 = bf16[4096,1024]{1,0:T(8,128)(2,1)} copy(bf16[4096,1024]{1,0:T(8,128)(2,1)} %get-tuple-element.6) | data formatting | bytes 16777216

commit v3 on v2

--- a/solution.py
+++ b/solution.py
@@ -60,15 +60,6 @@
     hid = trunk_hbm.shape[1]
     all_rows = task_count * rows
 
-    def partner(distance):
-        if width_count & (width_count - 1):
-            return lax.rem(wide + distance, width_count)
-        peer = wide
-        for bit in range(width_count.bit_length() - 1):
-            if (distance >> bit) & 1:
-                peer = peer + (1 << bit) * (1 - 2 * lax.rem(wide // (1 << bit), 2))
-        return peer
-
     def target(source_task, source_wide, step):
         place = (source_task * width_count + source_wide) * inner + step * step_cols
         return factors.at[
@@ -88,8 +79,8 @@
         )
 
     def send_wide(blocks, source_task, step):
-        for d in reversed(range(1, width_count)):
-            peer = partner(d)
+        for d in range(1, width_count):
+            peer = lax.rem(wide + d, width_count)
             pltpu.make_async_remote_copy(
                 src_ref=blocks.at[peer],
                 dst_ref=target(source_task, wide, step),
@@ -110,12 +101,19 @@
                 hop_copy(t, t, step).wait_recv()
                 send_wide(stage.at[t, step], t, step)
 
-    def forward_all(sources, first):
-        def body(step, carry):
-            forward(sources, step)
-            return carry
-
-        lax.fori_loop(first, steps, body, 0)
+    def wait_sent(sources, step):
+        for t in sources:
+            sent = stage.at[t, step, pl.ds(0, width_count - 1)]
+            pltpu.make_async_copy(sent, sent, wide_send.at[t, step]).wait()
+
+    def forward_entry(step, carry):
+        forward(entry_tasks, step)
+        return carry
+
+    def forward_exit(step, carry):
+        wait_sent(entry_tasks, step)
+        forward(exit_tasks, step)
+        return carry
 
     def wait_wide(sources, step):
         for t in sources:
@@ -128,9 +126,6 @@
             return carry
 
         lax.fori_loop(0, steps, body, 0)
-
-    lag = 5
-    early = max(0, steps - lag)
 
     def generate(table, trunk, one_hot, hidden, weight, perm, flat):
         def weight_copy(step):
@@ -232,12 +227,6 @@
             for d in range(1, task_count):
                 hop_copy(lax.rem(task + d, task_count), task, step).start()
             send_wide(outgoing.at[step, task], task, step)
-            if early:
-
-                @pl.when(step >= lag)
-                def _():
-                    forward(entry_tasks, step - lag)
-
             return carry
 
         lax.fori_loop(0, steps, head_step, 0)
@@ -252,9 +241,26 @@
         pltpu.VMEM((cols, cols), BF16),
         pltpu.VMEM((all_rows, cols), BF16),
     )
-    forward_all(entry_tasks, early)
-    forward_all(exit_tasks, 0)
-    wait_wide_all(entry_tasks)
+    lax.fori_loop(0, steps, forward_entry, 0)
+    lax.fori_loop(0, steps, forward_exit, 0)
+
+    chunk = min(256, slice_width)
+    aligned = inner % slice_width == 0 and chunk % step_cols == 0
+    count = slice_width // chunk
+
+    def columns(array, index):
+        return array.at[:, pl.ds(pl.multiple_of(index * chunk, chunk), chunk)]
+
+    def factor_columns(first, index):
+        return factors.at[
+            pl.ds(first, RANK), :, pl.ds(pl.multiple_of(index * chunk, chunk), chunk)
+        ]
+
+    def wait_columns(sources, index):
+        per = chunk // step_cols
+        for turn in range(inner // slice_width):
+            for q in range(per):
+                wait_wide(sources, turn * (slice_width // step_cols) + index * per + q)
 
     def part_copy(peer, slot):
         return pltpu.make_async_remote_copy(
@@ -268,51 +274,62 @@
 
     def rank(entry, tokens):
         def token_copy(index):
+            slot = lax.rem(index, 2)
             return pltpu.make_async_copy(
-                inputs_hbm.at[pl.ds(pl.multiple_of(index * block, block), block)],
-                tokens.at[lax.rem(index, 2)],
-                token_sem.at[lax.rem(index, 2)],
+                columns(inputs_hbm, index), tokens.at[slot], token_sem.at[slot]
             )
 
         token_copy(0).start()
-        entry_copy = pltpu.make_async_copy(factors.at[pl.ds(0, RANK)], entry, load_sem.at[0])
-        entry_copy.start()
-        entry_copy.wait()
-
-        def score_block(index, carry):
-            token_copy(index).wait()
-
-            @pl.when(index + 1 < width_count)
+        part[...] = jnp.zeros_like(part)
+        if not aligned:
+            wait_wide_all(entry_tasks)
+
+        def score_piece(index, carry):
+            slot = lax.rem(index, 2)
+
+            @pl.when(index + 1 < count)
             def _():
                 token_copy(index + 1).start()
 
-            local = token_ref[index] - task * rows
-            chosen = lax.broadcasted_iota(jnp.int32, (rows, block), 0) == local
-            block_in = tokens[lax.rem(index, 2)]
-            half = RANK // 2
-            for top in range(0, RANK, half):
-                scores = lax.dot_general(
-                    entry[top : top + half].reshape(half * rows, slice_width),
-                    block_in,
-                    (((1,), (1,)), ((), ())),
-                    preferred_element_type=F32,
-                ).reshape(half, rows, block)
-                part[index, top : top + half] = jnp.sum(
-                    jnp.where(chosen[None], scores, 0.0), axis=1
-                )
-
-            @pl.when(index != wide)
-            def _():
-                part_copy(index, wide).start()
-
+            if aligned:
+                wait_columns(entry_tasks, index)
+            entry_copy = pltpu.make_async_copy(factor_columns(0, index), entry, load_sem.at[0])
+            entry_copy.start()
+            token_copy(index).wait()
+            entry_copy.wait()
+
+            def score_block(row_block, inner_carry):
+                local = token_ref[row_block] - task * rows
+                chosen = lax.broadcasted_iota(jnp.int32, (rows, block), 0) == local
+                place = pl.ds(pl.multiple_of(row_block * block, block), block)
+                block_in = tokens[slot, place, :]
+                half = RANK // 2
+                for top in range(0, RANK, half):
+                    scores = lax.dot_general(
+                        entry[top : top + half].reshape(half * rows, chunk),
+                        block_in,
+                        (((1,), (1,)), ((), ())),
+                        preferred_element_type=F32,
+                    ).reshape(half, rows, block)
+                    part[row_block, top : top + half] += jnp.sum(
+                        jnp.where(chosen[None], scores, 0.0), axis=1
+                    )
+
+                @pl.when(jnp.logical_and(index == count - 1, row_block != wide))
+                def _():
+                    part_copy(row_block, wide).start()
+
+                return inner_carry
+
+            lax.fori_loop(0, width_count, score_block, 0)
             return carry
 
-        lax.fori_loop(0, width_count, score_block, 0)
+        lax.fori_loop(0, count, score_piece, 0)
 
     pl.run_scoped(
         rank,
-        pltpu.VMEM((RANK, rows, slice_width), BF16),
-        pltpu.VMEM((2, block, slice_width), BF16),
+        pltpu.VMEM((RANK, rows, chunk), BF16),
+        pltpu.VMEM((2, width_count * block, chunk), BF16),
     )
     total = part[wide]
     for d in range(1, width_count):
@@ -336,13 +353,7 @@
     for d in range(1, width_count):
         peer = lax.rem(wide + d, width_count)
         coef_copy(peer, peer).wait_recv()
-    chunk = min(256, slice_width)
-    aligned = inner % slice_width == 0 and chunk % step_cols == 0
-
     def update(spread, exit_buf, frozen_buf, out_buf):
-        def columns(array, index):
-            return array.at[:, pl.ds(pl.multiple_of(index * chunk, chunk), chunk)]
-
         def frozen_copy(index):
             slot = lax.rem(index, 2)
             return pltpu.make_async_copy(
@@ -369,7 +380,6 @@
             return carry
 
         lax.fori_loop(0, width_count, spread_block, 0)
-        count = slice_width // chunk
         if not aligned:
             wait_wide_all(exit_tasks)
 
@@ -381,18 +391,9 @@
                 frozen_copy(index + 1).start()
 
             if aligned:
-                per = chunk // step_cols
-                for turn in range(inner // slice_width):
-                    for q in range(per):
-                        wait_wide(
-                            exit_tasks, turn * (slice_width // step_cols) + index * per + q
-                        )
+                wait_columns(exit_tasks, index)
             exit_copy = pltpu.make_async_copy(
-                factors.at[
-                    pl.ds(RANK, RANK), :, pl.ds(pl.multiple_of(index * chunk, chunk), chunk)
-                ],
-                exit_buf,
-                load_sem.at[1],
+                factor_columns(RANK, index), exit_buf, load_sem.at[1]
             )
             exit_copy.start()
             frozen_copy(index).wait()
@@ -440,9 +441,7 @@
     def drain(step, carry):
         for d in range(1, task_count):
             hop_copy(lax.rem(task + d, task_count), task, step).wait_send()
-        for t in range(task_count):
-            sent = stage.at[t, step, pl.ds(0, width_count - 1)]
-            pltpu.make_async_copy(sent, sent, wide_send.at[t, step]).wait()
+        wait_sent(exit_tasks, step)
         return carry
 
     lax.fori_loop(0, steps, drain, 0)

time: 264 us -> 264 us (level)
  no operation moved by 1% of the time
where the time goes in v3:
time: 264 us
  Pallas kernels  256 us (97%)
  local copies, waits for them, and re-layouts  7.76 us (3%)
    pallas_call x1, Pallas kernels, on_device(): pl.pallas_call(functools.partial(exchange_kernel, dims), out_shape=(jax.S...  256 us
    unnamed x1, local copies, waits for them, and re-layouts  7.76 us

profile of v3, /device:TPU:0, one launch (start us, length us, event | category | flops | bytes accessed | tf_op | source)
XLA Modules:
  0.0 264.0 jit_solution(5301463051024038439)
XLA Ops:
  0.0 256.2 %adapt_rows.1 = (bf16[4096,1024]{1,0:T(8,128)(2,1)}, bf16[32,128,1024]{2,1,0:T(8,128)(2,1)}) custom-call(s32[1,128]{1,0:T(1,128)} %bitcast.7, bf16[1024,1024]{1,0:T(8,128)(2,1)} %table_hbm.1, bf16[1024,2048]{1,0:T(8,128)(2,1)} %trunk_hbm.1, f32[1,2048]{1,0:T(1,128)} %bitcast.6, bf16[2048,8192]{1,0:T(8,128)(2,1)} %head_hbm.1, f32[8,1,1024]{2,1,0:T(1,128)} %bitcast.4, ...), custom_call_target="tpu_custom_call" | custom-call | tf_op jit(solution)/shard_map/adapt_rows/pallas_call | solution.py:476
  256.2 7.8 %copy.11 = bf16[4096,1024]{1,0:T(8,128)(2,1)} copy(bf16[4096,1024]{1,0:T(8,128)(2,1)} %get-tuple-element.6) | data formatting | bytes 16777216

commit v4 on v3

--- a/solution.py
+++ b/solution.py
@@ -25,8 +25,7 @@
     head_bias_ref,
     token_ref,
     inputs_hbm,
-    frozen_hbm,
-    out_hbm,
+    spread_hbm,
     factors,
     ids_all,
     outgoing,
@@ -47,8 +46,7 @@
     load_sem,
     weight_sem,
     token_sem,
-    frozen_sem,
-    out_sem,
+    spread_sem,
 ):
     task_count, width_count, rows, inner, slice_width, step_cols, steps, block = dims
     cols = step_cols * width_count
@@ -353,85 +351,35 @@
     for d in range(1, width_count):
         peer = lax.rem(wide + d, width_count)
         coef_copy(peer, peer).wait_recv()
-    def update(spread, exit_buf, frozen_buf, out_buf):
-        def frozen_copy(index):
+    def spread_out(buffer):
+        def spread_copy(index):
             slot = lax.rem(index, 2)
             return pltpu.make_async_copy(
-                columns(frozen_hbm, index), frozen_buf.at[slot], frozen_sem.at[slot]
-            )
-
-        def out_copy(index):
-            slot = lax.rem(index, 2)
-            return pltpu.make_async_copy(
-                out_buf.at[slot], columns(out_hbm, index), out_sem.at[slot]
-            )
-
-        frozen_copy(0).start()
+                buffer.at[slot],
+                spread_hbm.at[pl.ds(pl.multiple_of(index * block, block), block)],
+                spread_sem.at[slot],
+            )
 
         def spread_block(index, carry):
+            @pl.when(index >= 2)
+            def _():
+                spread_copy(index - 2).wait()
+
             local = token_ref[index] - task * rows
             spread_ids = jnp.transpose(jnp.broadcast_to(local, (128, block)))
             chosen = spread_ids == lax.broadcasted_iota(jnp.int32, (block, 128), 1)
             coef = jnp.transpose(coef_all[index].astype(F32))
-            place = pl.ds(pl.multiple_of(index * block, block), block)
             for r in range(RANK):
                 piece = jnp.where(chosen, coef[:, r : r + 1], 0.0).astype(BF16)
-                spread[place, r * rows : (r + 1) * rows] = piece[:, :rows]
+                buffer[lax.rem(index, 2), :, r * rows : (r + 1) * rows] = piece[:, :rows]
+            spread_copy(index).start()
             return carry
 
         lax.fori_loop(0, width_count, spread_block, 0)
-        if not aligned:
-            wait_wide_all(exit_tasks)
-
-        def update_chunk(index, carry):
-            slot = lax.rem(index, 2)
-
-            @pl.when(index + 1 < count)
-            def _():
-                frozen_copy(index + 1).start()
-
-            if aligned:
-                wait_columns(exit_tasks, index)
-            exit_copy = pltpu.make_async_copy(
-                factor_columns(RANK, index), exit_buf, load_sem.at[1]
-            )
-            exit_copy.start()
-            frozen_copy(index).wait()
-
-            @pl.when(index >= 2)
-            def _():
-                out_copy(index - 2).wait()
-
-            exit_copy.wait()
-
-            def token_block(row_block, inner_carry):
-                place = pl.ds(pl.multiple_of(row_block * block, block), block)
-                change = jnp.dot(
-                    spread[place, :],
-                    exit_buf[...].reshape(RANK * rows, chunk),
-                    preferred_element_type=F32,
-                )
-                out_buf[slot, place, :] = (
-                    frozen_buf[slot, place, :].astype(F32) + change * (1.0 / math.sqrt(RANK))
-                ).astype(BF16)
-                return inner_carry
-
-            lax.fori_loop(0, width_count, token_block, 0)
-            out_copy(index).start()
-            return carry
-
-        lax.fori_loop(0, count, update_chunk, 0)
-        for index in range(max(0, count - 2), count):
-            out_copy(index).wait()
-
-    tok_count = width_count * block
-    pl.run_scoped(
-        update,
-        pltpu.VMEM((tok_count, RANK * rows), BF16),
-        pltpu.VMEM((RANK, rows, chunk), BF16),
-        pltpu.VMEM((2, tok_count, chunk), BF16),
-        pltpu.VMEM((2, tok_count, chunk), BF16),
-    )
+        for index in range(max(0, width_count - 2), width_count):
+            spread_copy(index).wait()
+
+    pl.run_scoped(spread_out, pltpu.VMEM((2, block, RANK * rows), BF16))
 
     for d in range(1, width_count):
         peer = lax.rem(wide + d, width_count)
@@ -445,6 +393,20 @@
         return carry
 
     lax.fori_loop(0, steps, drain, 0)
+    wait_wide_all(exit_tasks)
+
+
+def update_kernel(spread_ref, exit_ref, frozen_ref, out_ref):
+    slice_width = exit_ref.shape[2]
+    exit_flat = exit_ref[...].reshape(spread_ref.shape[1], slice_width)
+    tile = min(512, slice_width)
+    for k in range(0, slice_width, tile):
+        update = jnp.dot(
+            spread_ref[...], exit_flat[:, k : k + tile], preferred_element_type=F32
+        )
+        out_ref[:, k : k + tile] = (
+            frozen_ref[:, k : k + tile].astype(F32) + update * (1.0 / math.sqrt(RANK))
+        ).astype(BF16)
 
 
 def on_device(
@@ -473,13 +435,13 @@
     vmem = pl.BlockSpec(memory_space=pltpu.VMEM)
     hbm = pl.BlockSpec(memory_space=pl.ANY)
     dma = pltpu.SemaphoreType.DMA
-    out, _ = pl.pallas_call(
+    spread, factors = pl.pallas_call(
         functools.partial(exchange_kernel, dims),
         out_shape=(
-            jax.ShapeDtypeStruct((tok_count, slice_width), BF16),
+            jax.ShapeDtypeStruct((tok_count, RANK * rows), BF16),
             jax.ShapeDtypeStruct((2 * RANK, rows, slice_width), BF16),
         ),
-        in_specs=[vmem, hbm, hbm, vmem, hbm, vmem, vmem, hbm, hbm],
+        in_specs=[vmem, hbm, hbm, vmem, hbm, vmem, vmem, hbm],
         out_specs=(hbm, hbm),
         scratch_shapes=[
             pltpu.VMEM((task_count, 8, rows), jnp.int32),
@@ -502,7 +464,6 @@
             dma((2,)),
             dma((2,)),
             dma((2,)),
-            dma((2,)),
         ],
         compiler_params=pltpu.CompilerParams(
             collective_id=0, has_side_effects=True, vmem_limit_bytes=58 * 1024 * 1024
@@ -517,9 +478,20 @@
         head_bias.reshape(steps, 1, cols),
         token_blocks,
         inputs,
-        frozen,
     )
-    return out
+    return pl.pallas_call(
+        update_kernel,
+        grid=(width_count,),
+        out_shape=jax.ShapeDtypeStruct((tok_count, slice_width), BF16),
+        in_specs=[
+            pl.BlockSpec((block, RANK * rows), lambda i: (i, 0)),
+            pl.BlockSpec((RANK, rows, slice_width), lambda i: (1, 0, 0)),
+            pl.BlockSpec((block, slice_width), lambda i: (i, 0)),
+        ],
+        out_specs=pl.BlockSpec((block, slice_width), lambda i: (i, 0)),
+        compiler_params=pltpu.CompilerParams(vmem_limit_bytes=48 * 1024 * 1024),
+        name="apply_update",
+    )(spread, factors, frozen)
 
 
 def solution(mesh):

time: 264 us -> 249 us (0.943)
  Pallas kernels: 256 us -> 248 us
  local copies, waits for them, and re-layouts: 7.76 us -> 0 us
    pallas_call x1, Pallas kernels: 256 us -> 225 us  [on_device(): pl.pallas_call(functools.partial(exchange_kernel, dims), out_shape=(jax.S...]
    pallas_call x0 -> x1, Pallas kernels: none -> 23 us  [on_device(): pl.pallas_call(update_kernel, grid=(width_count,), out_shape=jax.ShapeDty...]
    unnamed x1 -> x0, local copies, waits for them, and re-layouts: 7.76 us -> none
where the time goes in v4:
time: 249 us; the launch traced here: 248 us
  Pallas kernels  248 us (100%)
    pallas_call x1, Pallas kernels, on_device(): pl.pallas_call(functools.partial(exchange_kernel, dims), out_shape=(jax.S...  225 us
    pallas_call x1, Pallas kernels, on_device(): pl.pallas_call(update_kernel, grid=(width_count,), out_shape=jax.ShapeDty...  23 us

profile of v4, /device:TPU:0, one launch (start us, length us, event | category | flops | bytes accessed | tf_op | source)
XLA Modules:
  0.0 248.3 jit_solution(8820948667365154093)
XLA Ops:
  0.0 225.3 %adapt_rows.1 = (bf16[4096,2048]{1,0:T(8,128)(2,1)}, bf16[32,128,1024]{2,1,0:T(8,128)(2,1)}) custom-call(s32[1,128]{1,0:T(1,128)} %bitcast.7, bf16[1024,1024]{1,0:T(8,128)(2,1)} %table_hbm.1, bf16[1024,2048]{1,0:T(8,128)(2,1)} %trunk_hbm.1, f32[1,2048]{1,0:T(1,128)} %bitcast.6, bf16[2048,8192]{1,0:T(8,128)(2,1)} %head_hbm.1, f32[8,1,1024]{2,1,0:T(1,128)} %bitcast.4, ...), custom_call_target="tpu_custom_call" | custom-call | tf_op jit(solution)/shard_map/adapt_rows/pallas_call | solution.py:438
  225.3 23.0 %apply_update.1 = bf16[4096,1024]{1,0:T(8,128)(2,1)} custom-call(bf16[4096,2048]{1,0:T(8,128)(2,1)} %get-tuple-element.7.spread_ref, bf16[32,128,1024]{2,1,0:T(8,128)(2,1)} %get-tuple-element.8.exit_ref, bf16[4096,1024]{1,0:T(8,128)(2,1)} %frozen_ref.1), custom_call_target="tpu_custom_call" | custom-call | tf_op jit(solution)/shard_map/apply_update/pallas_call | solution.py:482
